TPU v7x, 32 devices: a whole 2x2x4 slice. The times are simulated.
32 devices in a mesh: lag: 4 (over y, x), row: 8 (over z, core).
Axes of the slice: x: 2, y: 2, z: 4, core: 2. Of those that a mesh axis runs over, the one named last changes fastest.
Arguments:
- newest: bfloat16 [512, 8192], P('lag', 'row'), may hold values from -6 to 6
- earlier: bfloat16 [3, 8192], P(None, 'row'), may hold values from -6 to 6
- lag_matrices: bfloat16 [4, 8192, 8192], P('lag', 'row'), may hold values from -0.03125 to 0.03125
Outputs:
- forces: float32 [512, 8192], P('lag', 'row')
All inputs are finite; a program needn't handle non-finite values.
Results may differ from a plain program's by a relative error of at most 0.0003.
Values may be sent and summed in bfloat16 or wider, within the bound.
A program may use at most 64 MiB of HBM per device.

v0:
```python
import jax
import jax.numpy as jnp
from jax import lax
from jax.experimental import pallas as pl
from jax.experimental.pallas import tpu as pltpu
from jax.sharding import PartitionSpec as P

MESH = pl.DeviceIdType.MESH
PAD = 16
NZ = 4


def product(window, matrix):
    return lax.dot_general(
        window, matrix, (((1,), (1,)), ((), ())), preferred_element_type=jnp.float32
    )


def on_device_general(newest, earlier, lag_matrices):
    lag_index = lax.axis_index("lag")
    matrix = lag_matrices[0]
    own_steps = newest.shape[0]
    earlier_rows = earlier.shape[0]
    wide_newest, wide_earlier = (
        lax.all_gather(newest, "row", axis=1, tiled=True),
        lax.all_gather(earlier, "row", axis=1, tiled=True),
    )
    history = lax.all_gather(wide_newest, "lag", axis=0, tiled=True)
    record = jnp.concatenate([wide_earlier, history], axis=0)
    window = lax.dynamic_slice_in_dim(
        record, jnp.int32(0) + earlier_rows - lag_index, own_steps * lax.axis_size("lag"), 0
    )
    return lax.psum_scatter(product(window, matrix), "lag", scatter_dimension=0, tiled=True)


def kernel(new_ref, ear_ref, mat_ref, out_ref,
           mat, hist, ebuf, acc, s_d, s_x, s_y, r_d, r_1, r_2,
           loc, zs, zr, xs, xr, ys, yr, ss, sr, es, er, fs, fr):
    lag, row = lax.axis_index("lag"), lax.axis_index("row")
    x, y = lag % 2, lag // 2
    z, core = row // 2, row % 2
    sib = row + 1 - 2 * core
    t0, tx, ty = lag, 2 * y + 1 - x, 2 * (1 - y) + x
    td = 2 * (1 - y) + 1 - x
    steps, width = new_ref.shape
    half = steps // 2
    x_dev, y_dev = {"lag": tx, "row": row}, {"lag": ty, "row": row}
    sib_dev = {"lag": lag, "row": sib}

    mat_copy = pltpu.make_async_copy(mat_ref.at[0], mat, loc.at[0])
    mat_copy.start()

    def rows(t, h, n):
        return pl.ds(pl.multiple_of(PAD + t * steps + h * half, 16), n)

    own_copy = pltpu.make_async_copy(new_ref, hist.at[row, rows(t0, 0, steps)], loc.at[1])
    own_copy.start()
    own_e = pltpu.make_async_copy(ear_ref, ebuf.at[row], loc.at[2])
    own_e.start()

    barrier = pltpu.get_barrier_semaphore()
    for dev in (x_dev, y_dev):
        pl.semaphore_signal(barrier, inc=1, device_id=dev, device_id_type=MESH)
    for j in range(1, 2 * NZ):
        pl.semaphore_signal(barrier, inc=1, device_id={"lag": lag, "row": (row + j) % (2 * NZ)},
                            device_id_type=MESH)
    pl.semaphore_wait(barrier, 2 * NZ + 1)

    def copy(src, dst, ssem, rsem, dev):
        return pltpu.make_async_remote_copy(
            src_ref=src, dst_ref=dst, send_sem=ssem, recv_sem=rsem, device_id=dev,
            device_id_type=MESH)

    def place(r, t, h, n):
        return hist.at[r, rows(t, h, n)]

    z_kind = ((t0, 0, steps), (tx, 0, half), (ty, 1, half))
    x_kind = ((t0, 0, half), (t0, 1, half), (ty, 1, half))
    y_kind = ((t0, 1, half), (t0, 0, half), (tx, 0, half))
    s_kind = tuple((t, 0, steps) for t in (t0, tx, ty, td))
    x_got = ((tx, 0, half), (tx, 1, half), (td, 1, half))
    y_got = ((ty, 1, half), (ty, 0, half), (td, 0, half))

    def fam(zz):
        return 2 * zz + core

    def z_msg(up, zz, m):
        dev = {"lag": lag, "row": row + 2 if up else row - 2}
        ref = place(fam(zz), *z_kind[m])
        return copy(ref, ref, zs.at[int(up), zz, m], zr.at[zz, m], dev)

    def z_own(up):
        dev = {"lag": lag, "row": row + 2 if up else row - 2}
        return copy(new_ref, place(row, *z_kind[0]), zs.at[int(up), z, 0], zr.at[z, 0], dev)

    def x_msg(zz, m):
        ref = place(fam(zz), *x_kind[m])
        return copy(ref, ref, xs.at[zz, m], xr.at[zz, m], x_dev)

    def y_msg(zz, m):
        ref = place(fam(zz), *y_kind[m])
        return copy(ref, ref, ys.at[zz, m], yr.at[zz, m], y_dev)

    def s_msg(zz, m):
        ref = place(fam(zz), *s_kind[m])
        return copy(ref, ref, ss.at[zz, m], sr.at[zz, m], sib_dev)

    def z_wait(zz, m):
        ref = place(fam(zz), *z_kind[m])
        copy(ref, ref, zs.at[0, zz, m], zr.at[zz, m], x_dev).wait_recv()

    def x_wait(zz, m):
        ref = place(fam(zz), *x_got[m])
        copy(ref, ref, xs.at[zz, m], xr.at[zz, m], x_dev).wait_recv()

    def y_wait(zz, m):
        ref = place(fam(zz), *y_got[m])
        copy(ref, ref, ys.at[zz, m], yr.at[zz, m], y_dev).wait_recv()

    def s_wait(zz, m):
        ref = place(2 * zz + 1 - core, *s_kind[m])
        copy(ref, ref, ss.at[zz, m], sr.at[zz, m], sib_dev).wait_recv()

    can_up, can_down = z < NZ - 1, z > 0

    def own_half(h):
        return new_ref.at[pl.ds(h * half, half)]

    @pl.when(can_up)
    def _():
        z_own(True).start()

    @pl.when(can_down)
    def _():
        z_own(False).start()

    own_x = [copy(own_half(h), place(row, t0, h, half), xs.at[z, h], xr.at[z, h], x_dev)
             for h in (0, 1)]
    own_y = [copy(own_half(1 - m), place(row, t0, 1 - m, half), ys.at[z, m], yr.at[z, m], y_dev)
             for m in (0, 1)]
    for m in (0, 1):
        own_x[m].start()
        own_y[m].start()
    copy(new_ref, place(row, t0, 0, steps), ss.at[z, 0], sr.at[z, 0], sib_dev).start()

    def e_msg(j):
        to = (row + j) % (2 * NZ)
        return copy(ear_ref, ebuf.at[row], es.at[j], er.at[row], {"lag": lag, "row": to})

    def e_wait(j):
        frm = (row + j) % (2 * NZ)
        copy(ear_ref, ebuf.at[frm], es.at[j], er.at[frm], sib_dev).wait_recv()

    for j in range(1, 2 * NZ):
        e_msg(j).start()

    wide_up, wide_down = z < NZ - 2, z > 1
    at_end = (z == 0) | (z == NZ - 1)

    def z_on_both(m):
        @pl.when(wide_up)
        def _():
            z_msg(True, z, m).start()

        @pl.when(wide_down)
        def _():
            z_msg(False, z, m).start()

    def arrive(zz, m, up):
        z_wait(zz, m)

        @pl.when(can_up if up else can_down)
        def _():
            z_msg(up, zz, m).start()

        if m == 0:
            x_msg(zz, 1).start()
            y_msg(zz, 1).start()
            s_msg(zz, 0).start()
        elif m == 1:
            y_msg(zz, 2).start()
        else:
            x_msg(zz, 2).start()

    def rest(zz):
        x_wait(zz, 1)
        s_msg(zz, 1).start()
        y_wait(zz, 1)
        s_msg(zz, 2).start()
        x_wait(zz, 2)
        y_wait(zz, 2)
        s_msg(zz, 3).start()

    wide = 512

    def add_plane(zz, n, first=False):
        total = None
        for c in range(2):
            r = 2 * zz + c
            cols = pl.ds(pl.multiple_of(r * width, width), width)
            term = product(hist[r], mat[n, cols])
            total = term if total is None else total + term
        if first:
            acc[:, n] = total
        else:
            acc[:, n] += total

    def whole(zz):
        for m in range(4):
            s_wait(zz, m)

    def some(zz, i, first=False):
        add_plane(zz, pl.ds(i * wide, wide), first)

    x_wait(z, 0)
    z_on_both(1)
    y_msg(z, 2).start()
    y_wait(z, 0)
    z_on_both(2)
    x_msg(z, 2).start()
    inner = jnp.where(z == 0, 1, NZ - 2)

    @pl.when(at_end)
    def _():
        z_wait(inner, 0)
        for m in (0, 1):
            x_msg(inner, m).start()
            y_msg(inner, m).start()
        s_msg(inner, 0).start()

    @pl.when(jnp.logical_not(at_end))
    def _():
        arrive(z - 1, 0, True)
        arrive(z + 1, 0, False)

    own_copy.wait()
    own_e.wait()
    rest(z)
    @pl.when(at_end)
    def _():
        x_wait(inner, 0)
        y_msg(inner, 2).start()
        y_wait(inner, 0)
        x_msg(inner, 2).start()

    @pl.when(jnp.logical_not(at_end))
    def _():
        for m in (1, 2):
            arrive(z - 1, m, True)
            arrive(z + 1, m, False)

    for j in range(1, 2 * NZ):
        e_wait(j)
    chunk = ear_ref.shape[1]
    for r in range(2 * NZ):
        e = ebuf[r].astype(jnp.float32)
        for j in range(width // chunk):
            cut = 4 * j + 4
            piece = e if cut == PAD else jnp.concatenate([e[cut:], e[:cut]], axis=0)
            hist[r, 0:PAD, j * chunk:(j + 1) * chunk] = piece.astype(hist.dtype)
    mat_copy.wait()
    whole(z)
    for i in range(2):
        some(z, i, first=True)
    low = z < NZ // 2
    last = jnp.where(low, NZ - 1, 0)

    def arrive_far(zz, m):
        z_wait(zz, m)
        if m == 0:
            x_msg(zz, 1).start()
            y_msg(zz, 1).start()
            s_msg(zz, 0).start()
        elif m == 1:
            y_msg(zz, 2).start()
        else:
            x_msg(zz, 2).start()

    @pl.when(at_end)
    def _():
        second = jnp.where(low, 2, NZ - 3)
        arrive_far(second, 0)
        rest(inner)
        arrive_far(second, 1)
        arrive_far(second, 2)
        whole(inner)
        for i in range(2):
            some(inner, i)
        arrive_far(last, 0)
        rest(second)
        whole(second)
        arrive_far(last, 1)
        arrive_far(last, 2)
        for i in range(2):
            some(second, i)

    @pl.when(jnp.logical_not(at_end))
    def _():
        def on(m):
            z_wait(last, m)

            @pl.when(low)
            def _():
                z_msg(False, last, m).start()

            @pl.when(jnp.logical_not(low))
            def _():
                z_msg(True, last, m).start()

            if m == 0:
                x_msg(last, 1).start()
                y_msg(last, 1).start()
                s_msg(last, 0).start()
            elif m == 1:
                y_msg(last, 2).start()
            else:
                x_msg(last, 2).start()

        on(0)
        rest(z - 1)
        rest(z + 1)
        on(1)
        whole(z - 1)
        some(z - 1, 0)
        on(2)
        some(z - 1, 1)
        whole(z + 1)
        for i in range(2):
            some(z + 1, i)

    rest(last)
    whole(last)

    tile = s_d.shape[2]
    tiles = width // tile

    def shifted(t, h, i):
        start = pl.multiple_of(PAD - 8 + t * steps + h * half, 8)
        part = acc[pl.ds(start, half + 8), i * tile:(i + 1) * tile]
        got = part[8:]
        for k in range(1, 4):
            got = jnp.where(lag == k, part[8 - k:8 - k + half], got)
        return got

    def f_msg(src, dst, h, i, j, dev):
        cut = pl.ds(h * half, half)
        return copy(src.at[i, cut], dst.at[i, cut], fs.at[j, i], fr.at[j, i], dev)

    lo, hi = slice(0, half), slice(half, steps)
    hop_y = [f_msg(s_d, r_d, 0, i, 0, y_dev) for i in range(tiles)]
    hop_x = [f_msg(s_d, r_d, 1, i, 1, x_dev) for i in range(tiles)]
    dir_x = [f_msg(s_x, r_1, 1, i, 2, x_dev) for i in range(tiles)]
    dir_y = [f_msg(s_y, r_1, 0, i, 3, y_dev) for i in range(tiles)]
    last_x = [f_msg(s_x, r_2, 0, i, 4, x_dev) for i in range(tiles)]
    last_y = [f_msg(s_y, r_2, 1, i, 5, y_dev) for i in range(tiles)]
    for i in range(tiles):
        add_plane(last, pl.ds(i * tile, tile))
        s_d[i, lo] = shifted(td, 0, i)
        hop_y[i].start()
        s_d[i, hi] = shifted(td, 1, i)
        hop_x[i].start()
        s_x[i, hi] = shifted(tx, 1, i)
        dir_x[i].start()
        s_y[i, lo] = shifted(ty, 0, i)
        dir_y[i].start()
    for i in range(tiles):
        part_x, part_y = shifted(tx, 0, i), shifted(ty, 1, i)
        hop_y[i].wait_recv()
        s_x[i, lo] = part_x + r_d[i, lo]
        last_x[i].start()
        hop_x[i].wait_recv()
        s_y[i, hi] = part_y + r_d[i, hi]
        last_y[i].start()
    for i in range(tiles):
        n = slice(i * tile, (i + 1) * tile)
        dir_x[i].wait_recv()
        dir_y[i].wait_recv()
        out_ref[lo, n] = shifted(t0, 0, i) + r_1[i, lo]
        out_ref[hi, n] = shifted(t0, 1, i) + r_1[i, hi]
    for i in range(tiles):
        n = slice(i * tile, (i + 1) * tile)
        last_x[i].wait_recv()
        out_ref[lo, n] += r_2[i, lo]
        last_y[i].wait_recv()
        out_ref[hi, n] += r_2[i, hi]

    for group in (hop_y, hop_x, dir_x, dir_y, last_x, last_y):
        for c in group:
            c.wait_send()
    for j in range(1, 2 * NZ):
        e_msg(j).wait_send()
    x_msg(z, 0).wait_send()
    y_msg(z, 0).wait_send()

    @pl.when(at_end)
    def _():
        x_msg(inner, 0).wait_send()
        y_msg(inner, 0).wait_send()

    for zz in range(NZ):
        for m in range(3):
            @pl.when(can_up & (z >= zz) & ((z != zz) | wide_up | (m == 0)))
            def _():
                z_msg(True, zz, m).wait_send()

            @pl.when(can_down & (z <= zz) & ((z != zz) | wide_down | (m == 0)))
            def _():
                z_msg(False, zz, m).wait_send()
        for m in (1, 2):
            x_msg(zz, m).wait_send()
            y_msg(zz, m).wait_send()
        for m in range(4):
            s_msg(zz, m).wait_send()


def on_device(newest, earlier, lag_matrices):
    steps, width = newest.shape
    height = lag_matrices.shape[1]
    count = earlier.shape[0]
    groups = PAD // 4
    packed = jnp.pad(earlier, ((4 - count, 0), (0, 0)))
    packed = packed.reshape(4, groups, width // groups).transpose(1, 0, 2).reshape(PAD, width // groups)
    any_spec = pl.BlockSpec(memory_space=pl.ANY)
    vmem = pl.BlockSpec(memory_space=pltpu.VMEM)
    dma = pltpu.SemaphoreType.DMA
    tile = 256
    block = pltpu.VMEM((height // tile, steps, tile), jnp.float32)
    return pl.pallas_call(
        kernel,
        out_shape=jax.ShapeDtypeStruct((steps, height), jnp.float32),
        in_specs=[any_spec, any_spec, any_spec],
        out_specs=vmem,
        scratch_shapes=[
            pltpu.VMEM((height, 2 * NZ * width), jnp.bfloat16),
            pltpu.VMEM((2 * NZ, PAD + 4 * steps, width), jnp.bfloat16),
            pltpu.VMEM((2 * NZ, PAD, width // groups), jnp.bfloat16),
            pltpu.VMEM((PAD + 4 * steps, height), jnp.float32),
            block, block, block, block, block, block,
            dma((3,)),
            dma((2, NZ, 3)), dma((NZ, 3)),
            dma((NZ, 3)), dma((NZ, 3)),
            dma((NZ, 3)), dma((NZ, 3)),
            dma((NZ, 4)), dma((NZ, 4)),
            dma((2 * NZ,)), dma((2 * NZ,)),
            dma((6, height // tile)), dma((6, height // tile)),
        ],
        compiler_params=pltpu.CompilerParams(
            collective_id=0, has_side_effects=True, vmem_limit_bytes=48 * 1024 * 1024
        ),
        cost_estimate=pl.CostEstimate(
            flops=2 * 4 * steps * height * 2 * NZ * width,
            bytes_accessed=height * 2 * NZ * width * 2, transcendentals=0),
    )(newest, packed, lag_matrices)


def solution(mesh):
    in_specs = (P("lag", "row"), P(None, "row"), P("lag", "row", None))
    out_specs = P("lag", "row")
    fits = mesh.shape["lag"] == 4 and mesh.shape["row"] == 2 * NZ
    return jax.shard_map(
        on_device if fits else on_device_general,
        mesh=mesh, in_specs=in_specs, out_specs=out_specs, check_vma=False
    )
```

profile of v0, /device:TPU:0, one launch (start us, length us, event | category | flops | bytes accessed | tf_op | source)
XLA Modules:
  0.0 66.8 jit_solution(3527776738194627274)
XLA Ops:
  0.0 0.7 %pad.4 = bf16[4,1024]{1,0:T(4,128)(2,1)S(1)} pad(bf16[3,1024]{1,0:T(4,128)(2,1)} %param.4, bf16[]{:T(256)} %constant.2.clone.1), padding=1_0x0_0 | pad | bytes 14338 | tf_op jit(solution)/shard_map/jit(_pad)/pad | solution.py:421
  0.7 0.0 copy-start
  0.7 0.9 %copy-done = bf16[128,1024]{1,0:T(8,128)(2,1)S(1)} copy-done((bf16[128,1024]{1,0:T(8,128)(2,1)S(1)}, bf16[128,1024]{1,0:T(8,128)(2,1)}, u32[]{:S(2)}) %copy-start) | copy-done | bytes 262168
  1.7 64.3 %shard_map.37 = f32[128,1024]{1,0:T(8,128)S(1)} custom-call(bf16[128,1024]{1,0:T(8,128)(2,1)S(1)} %copy-done, bf16[16,256]{1,0:T(8,128)(2,1)S(1)} %reshape.7.ear_ref, bf16[1,1024,8192]{2,1,0:T(8,128)(2,1)} %mat_ref.1), custom_call_target="tpu_custom_call" | custom-call | flops 8589934592 | bytes 16777216 | tf_op jit(solution)/shard_map/pallas_call | solution.py:428
  66.0 0.8 %copy.6 = f32[128,1024]{1,0:T(8,128)} copy(f32[128,1024]{1,0:T(8,128)S(1)} %shard_map.37) | data formatting | bytes 1048576
  (1 shorter events, 0.0 us)
Async XLA Ops:
  0.7 1.0 %copy-start = (bf16[128,1024]{1,0:T(8,128)(2,1)S(1)}, bf16[128,1024]{1,0:T(8,128)(2,1)}, u32[]{:S(2)}) copy-start(bf16[128,1024]{1,0:T(8,128)(2,1)} %new_ref.1) | copy-start | bytes 786436
where the time goes:
time: 67 us; the launch traced here: 66.8 us
  Pallas kernels  64.3 us (96%)
  local copies, waits for them, and re-layouts  2.46 us (4%)
    pallas_call x1, Pallas kernels, on_device(): pl.pallas_call(kernel, out_shape=jax.ShapeDtypeStruct((steps, height), jn...  64.3 us
    unnamed x3, local copies, waits for them, and re-layouts  1.74 us

commit v1 on v0

--- a/solution.py
+++ b/solution.py
@@ -44,16 +44,17 @@
     td = 2 * (1 - y) + 1 - x
     steps, width = new_ref.shape
     half = steps // 2
+    quarter = steps // 4
     x_dev, y_dev = {"lag": tx, "row": row}, {"lag": ty, "row": row}
     sib_dev = {"lag": lag, "row": sib}
 
     mat_copy = pltpu.make_async_copy(mat_ref.at[0], mat, loc.at[0])
     mat_copy.start()
 
-    def rows(t, h, n):
-        return pl.ds(pl.multiple_of(PAD + t * steps + h * half, 16), n)
-
-    own_copy = pltpu.make_async_copy(new_ref, hist.at[row, rows(t0, 0, steps)], loc.at[1])
+    def rows(t, q, n):
+        return pl.ds(pl.multiple_of(PAD + t * steps + q * quarter, 16), n * quarter)
+
+    own_copy = pltpu.make_async_copy(new_ref, hist.at[row, rows(t0, 0, 4)], loc.at[1])
     own_copy.start()
     own_e = pltpu.make_async_copy(ear_ref, ebuf.at[row], loc.at[2])
     own_e.start()
@@ -71,15 +72,15 @@
             src_ref=src, dst_ref=dst, send_sem=ssem, recv_sem=rsem, device_id=dev,
             device_id_type=MESH)
 
-    def place(r, t, h, n):
-        return hist.at[r, rows(t, h, n)]
-
-    z_kind = ((t0, 0, steps), (tx, 0, half), (ty, 1, half))
-    x_kind = ((t0, 0, half), (t0, 1, half), (ty, 1, half))
-    y_kind = ((t0, 1, half), (t0, 0, half), (tx, 0, half))
-    s_kind = tuple((t, 0, steps) for t in (t0, tx, ty, td))
-    x_got = ((tx, 0, half), (tx, 1, half), (td, 1, half))
-    y_got = ((ty, 1, half), (ty, 0, half), (td, 0, half))
+    def place(r, t, q, n):
+        return hist.at[r, rows(t, q, n)]
+
+    z_kind = ((t0, 0, 2), (t0, 2, 2), (tx, 0, 1), (ty, 2, 1), (tx, 1, 1), (ty, 3, 1))
+    x_kind = ((t0, 0, 2), (t0, 2, 2), (ty, 2, 1), (ty, 3, 1))
+    y_kind = ((t0, 2, 2), (t0, 0, 2), (tx, 0, 1), (tx, 1, 1))
+    s_kind = tuple((t, 0, 4) for t in (t0, tx, ty, td))
+    x_got = ((tx, 0, 2), (tx, 2, 2), (td, 2, 1), (td, 3, 1))
+    y_got = ((ty, 2, 2), (ty, 0, 2), (td, 0, 1), (td, 1, 1))
 
     def fam(zz):
         return 2 * zz + core
@@ -89,9 +90,9 @@
         ref = place(fam(zz), *z_kind[m])
         return copy(ref, ref, zs.at[int(up), zz, m], zr.at[zz, m], dev)
 
-    def z_own(up):
+    def z_own(up, h):
         dev = {"lag": lag, "row": row + 2 if up else row - 2}
-        return copy(new_ref, place(row, *z_kind[0]), zs.at[int(up), z, 0], zr.at[z, 0], dev)
+        return copy(own_half(h), place(row, *z_kind[h]), zs.at[int(up), z, h], zr.at[z, h], dev)
 
     def x_msg(zz, m):
         ref = place(fam(zz), *x_kind[m])
@@ -126,22 +127,23 @@
     def own_half(h):
         return new_ref.at[pl.ds(h * half, half)]
 
-    @pl.when(can_up)
-    def _():
-        z_own(True).start()
-
-    @pl.when(can_down)
-    def _():
-        z_own(False).start()
-
-    own_x = [copy(own_half(h), place(row, t0, h, half), xs.at[z, h], xr.at[z, h], x_dev)
+    for h in (0, 1):
+        @pl.when(can_up)
+        def _():
+            z_own(True, h).start()
+
+        @pl.when(can_down)
+        def _():
+            z_own(False, h).start()
+
+    own_x = [copy(own_half(h), place(row, t0, 2 * h, 2), xs.at[z, h], xr.at[z, h], x_dev)
              for h in (0, 1)]
-    own_y = [copy(own_half(1 - m), place(row, t0, 1 - m, half), ys.at[z, m], yr.at[z, m], y_dev)
+    own_y = [copy(own_half(1 - m), place(row, t0, 2 - 2 * m, 2), ys.at[z, m], yr.at[z, m], y_dev)
              for m in (0, 1)]
     for m in (0, 1):
         own_x[m].start()
         own_y[m].start()
-    copy(new_ref, place(row, t0, 0, steps), ss.at[z, 0], sr.at[z, 0], sib_dev).start()
+    copy(new_ref, place(row, t0, 0, 4), ss.at[z, 0], sr.at[z, 0], sib_dev).start()
 
     def e_msg(j):
         to = (row + j) % (2 * NZ)
@@ -166,6 +168,14 @@
         def _():
             z_msg(False, z, m).start()
 
+    def share(zz, m):
+        if m % 2 == 0:
+            y_msg(zz, 1 + m // 2).start()
+        else:
+            x_msg(zz, 1 + m // 2).start()
+        if m == 1:
+            s_msg(zz, 0).start()
+
     def arrive(zz, m, up):
         z_wait(zz, m)
 
@@ -173,22 +183,16 @@
         def _():
             z_msg(up, zz, m).start()
 
-        if m == 0:
-            x_msg(zz, 1).start()
-            y_msg(zz, 1).start()
-            s_msg(zz, 0).start()
-        elif m == 1:
-            y_msg(zz, 2).start()
-        else:
-            x_msg(zz, 2).start()
+        share(zz, m)
 
     def rest(zz):
         x_wait(zz, 1)
         s_msg(zz, 1).start()
         y_wait(zz, 1)
         s_msg(zz, 2).start()
-        x_wait(zz, 2)
-        y_wait(zz, 2)
+        for m in (2, 3):
+            x_wait(zz, m)
+            y_wait(zz, m)
         s_msg(zz, 3).start()
 
     wide = 512
@@ -212,27 +216,35 @@
     def some(zz, i, first=False):
         add_plane(zz, pl.ds(i * wide, wide), first)
 
+    inner = jnp.where(z == 0, 1, NZ - 2)
+    between = jnp.logical_not(at_end)
+
+    def beside(m):
+        @pl.when(at_end)
+        def _():
+            z_wait(inner, m)
+            x_msg(inner, m).start()
+            y_msg(inner, 1 - m).start()
+            if m == 1:
+                s_msg(inner, 0).start()
+
+        @pl.when(between)
+        def _():
+            arrive(z - 1, m, True)
+            arrive(z + 1, m, False)
+
+    beside(0)
     x_wait(z, 0)
-    z_on_both(1)
+    z_on_both(2)
     y_msg(z, 2).start()
     y_wait(z, 0)
-    z_on_both(2)
+    z_on_both(3)
     x_msg(z, 2).start()
-    inner = jnp.where(z == 0, 1, NZ - 2)
-
-    @pl.when(at_end)
-    def _():
-        z_wait(inner, 0)
-        for m in (0, 1):
-            x_msg(inner, m).start()
-            y_msg(inner, m).start()
-        s_msg(inner, 0).start()
-
-    @pl.when(jnp.logical_not(at_end))
-    def _():
-        arrive(z - 1, 0, True)
-        arrive(z + 1, 0, False)
-
+    z_on_both(4)
+    y_msg(z, 3).start()
+    z_on_both(5)
+    x_msg(z, 3).start()
+    beside(1)
     own_copy.wait()
     own_e.wait()
     rest(z)
@@ -242,10 +254,12 @@
         y_msg(inner, 2).start()
         y_wait(inner, 0)
         x_msg(inner, 2).start()
-
-    @pl.when(jnp.logical_not(at_end))
+        y_msg(inner, 3).start()
+        x_msg(inner, 3).start()
+
+    @pl.when(between)
     def _():
-        for m in (1, 2):
+        for m in range(2, 6):
             arrive(z - 1, m, True)
             arrive(z + 1, m, False)
 
@@ -265,68 +279,53 @@
     low = z < NZ // 2
     last = jnp.where(low, NZ - 1, 0)
 
-    def arrive_far(zz, m):
-        z_wait(zz, m)
-        if m == 0:
-            x_msg(zz, 1).start()
-            y_msg(zz, 1).start()
-            s_msg(zz, 0).start()
-        elif m == 1:
-            y_msg(zz, 2).start()
-        else:
-            x_msg(zz, 2).start()
-
     @pl.when(at_end)
     def _():
         second = jnp.where(low, 2, NZ - 3)
-        arrive_far(second, 0)
+
+        def far(zz, *ms):
+            for m in ms:
+                z_wait(zz, m)
+                share(zz, m)
+
+        far(second, 0, 1, 2, 3)
         rest(inner)
-        arrive_far(second, 1)
-        arrive_far(second, 2)
+        far(second, 4, 5)
         whole(inner)
         for i in range(2):
             some(inner, i)
-        arrive_far(last, 0)
+        far(last, 0, 1)
         rest(second)
+        far(last, 2, 3)
         whole(second)
-        arrive_far(last, 1)
-        arrive_far(last, 2)
-        for i in range(2):
-            some(second, i)
-
-    @pl.when(jnp.logical_not(at_end))
+        some(second, 0)
+        far(last, 4, 5)
+        some(second, 1)
+
+    @pl.when(between)
     def _():
-        def on(m):
-            z_wait(last, m)
-
-            @pl.when(low)
-            def _():
-                z_msg(False, last, m).start()
-
-            @pl.when(jnp.logical_not(low))
-            def _():
-                z_msg(True, last, m).start()
-
-            if m == 0:
-                x_msg(last, 1).start()
-                y_msg(last, 1).start()
-                s_msg(last, 0).start()
-            elif m == 1:
-                y_msg(last, 2).start()
-            else:
-                x_msg(last, 2).start()
-
-        on(0)
+        def on(*ms):
+            for m in ms:
+                z_wait(last, m)
+
+                @pl.when(low)
+                def _():
+                    z_msg(False, last, m).start()
+
+                @pl.when(jnp.logical_not(low))
+                def _():
+                    z_msg(True, last, m).start()
+
+                share(last, m)
+
+        on(0, 1, 2, 3)
         rest(z - 1)
         rest(z + 1)
-        on(1)
-        whole(z - 1)
-        some(z - 1, 0)
-        on(2)
-        some(z - 1, 1)
-        whole(z + 1)
-        for i in range(2):
-            some(z + 1, i)
+        on(4, 5)
+        for zz in (z - 1, z + 1):
+            whole(zz)
+            for i in range(2):
+                some(zz, i)
 
     rest(last)
     whole(last)
@@ -398,15 +397,15 @@
         y_msg(inner, 0).wait_send()
 
     for zz in range(NZ):
-        for m in range(3):
-            @pl.when(can_up & (z >= zz) & ((z != zz) | wide_up | (m == 0)))
+        for m in range(6):
+            @pl.when(can_up & (z >= zz) & ((z != zz) | wide_up | (m < 2)))
             def _():
                 z_msg(True, zz, m).wait_send()
 
-            @pl.when(can_down & (z <= zz) & ((z != zz) | wide_down | (m == 0)))
+            @pl.when(can_down & (z <= zz) & ((z != zz) | wide_down | (m < 2)))
             def _():
                 z_msg(False, zz, m).wait_send()
-        for m in (1, 2):
+        for m in (1, 2, 3):
             x_msg(zz, m).wait_send()
             y_msg(zz, m).wait_send()
         for m in range(4):
@@ -428,7 +427,7 @@
     return pl.pallas_call(
         kernel,
         out_shape=jax.ShapeDtypeStruct((steps, height), jnp.float32),
-        in_specs=[any_spec, any_spec, any_spec],
+        in_specs=[pl.BlockSpec(memory_space=pltpu.HBM), any_spec, any_spec],
         out_specs=vmem,
         scratch_shapes=[
             pltpu.VMEM((height, 2 * NZ * width), jnp.bfloat16),
@@ -437,9 +436,9 @@
             pltpu.VMEM((PAD + 4 * steps, height), jnp.float32),
             block, block, block, block, block, block,
             dma((3,)),
-            dma((2, NZ, 3)), dma((NZ, 3)),
-            dma((NZ, 3)), dma((NZ, 3)),
-            dma((NZ, 3)), dma((NZ, 3)),
+            dma((2, NZ, 6)), dma((NZ, 6)),
+            dma((NZ, 4)), dma((NZ, 4)),
+            dma((NZ, 4)), dma((NZ, 4)),
             dma((NZ, 4)), dma((NZ, 4)),
             dma((2 * NZ,)), dma((2 * NZ,)),
             dma((6, height // tile)), dma((6, height // tile)),

time: 67 us -> 67.7 us (1.010)
  no operation moved by 1% of the time
where the time goes in v1:
time: 67.7 us; the launch traced here: 67.4 us
  Pallas kernels  64.9 us (96%)
  local copies, waits for them, and re-layouts  2.46 us (4%)
    pallas_call x1, Pallas kernels, on_device(): pl.pallas_call(kernel, out_shape=jax.ShapeDtypeStruct((steps, height), jn...  64.9 us
    unnamed x3, local copies, waits for them, and re-layouts  1.74 us

profile of v1, /device:TPU:0, one launch (start us, length us, event | category | flops | bytes accessed | tf_op | source)
XLA Modules:
  0.0 67.4 jit_solution(11706026305033805609)
XLA Ops:
  0.0 0.7 %pad.4 = bf16[4,1024]{1,0:T(4,128)(2,1)S(1)} pad(bf16[3,1024]{1,0:T(4,128)(2,1)} %param.4, bf16[]{:T(256)} %constant.2.clone.1), padding=1_0x0_0 | pad | bytes 14338 | tf_op jit(solution)/shard_map/jit(_pad)/pad | solution.py:420
  0.7 0.0 copy-start
  0.7 0.9 %copy-done = bf16[128,1024]{1,0:T(8,128)(2,1)S(1)} copy-done((bf16[128,1024]{1,0:T(8,128)(2,1)S(1)}, bf16[128,1024]{1,0:T(8,128)(2,1)}, u32[]{:S(2)}) %copy-start) | copy-done | bytes 262168
  1.7 64.9 %shard_map.37 = f32[128,1024]{1,0:T(8,128)S(1)} custom-call(bf16[128,1024]{1,0:T(8,128)(2,1)S(1)} %copy-done, bf16[16,256]{1,0:T(8,128)(2,1)S(1)} %reshape.7.ear_ref, bf16[1,1024,8192]{2,1,0:T(8,128)(2,1)} %mat_ref.1), custom_call_target="tpu_custom_call" | custom-call | flops 8589934592 | bytes 16777216 | tf_op jit(solution)/shard_map/pallas_call | solution.py:427
  66.6 0.8 %copy.6 = f32[128,1024]{1,0:T(8,128)} copy(f32[128,1024]{1,0:T(8,128)S(1)} %shard_map.37) | data formatting | bytes 1048576
  (1 shorter events, 0.0 us)
Async XLA Ops:
  0.7 1.0 %copy-start = (bf16[128,1024]{1,0:T(8,128)(2,1)S(1)}, bf16[128,1024]{1,0:T(8,128)(2,1)}, u32[]{:S(2)}) copy-start(bf16[128,1024]{1,0:T(8,128)(2,1)} %new_ref.1) | copy-start | bytes 786436

commit v2 on v0

--- a/solution.py
+++ b/solution.py
@@ -105,6 +105,14 @@
         ref = place(fam(zz), *s_kind[m])
         return copy(ref, ref, ss.at[zz, m], sr.at[zz, m], sib_dev)
 
+    def s_all(zz):
+        ref = hist.at[fam(zz), pl.ds(PAD, 4 * steps)]
+        return copy(ref, ref, ss.at[zz, 0], sr.at[zz, 0], sib_dev)
+
+    def s_all_wait(zz):
+        ref = hist.at[2 * zz + 1 - core, pl.ds(PAD, 4 * steps)]
+        copy(ref, ref, ss.at[zz, 0], sr.at[zz, 0], sib_dev).wait_recv()
+
     def z_wait(zz, m):
         ref = place(fam(zz), *z_kind[m])
         copy(ref, ref, zs.at[0, zz, m], zr.at[zz, m], x_dev).wait_recv()
@@ -141,7 +149,6 @@
     for m in (0, 1):
         own_x[m].start()
         own_y[m].start()
-    copy(new_ref, place(row, t0, 0, steps), ss.at[z, 0], sr.at[z, 0], sib_dev).start()
 
     def e_msg(j):
         to = (row + j) % (2 * NZ)
@@ -176,13 +183,18 @@
         if m == 0:
             x_msg(zz, 1).start()
             y_msg(zz, 1).start()
-            s_msg(zz, 0).start()
         elif m == 1:
             y_msg(zz, 2).start()
         else:
             x_msg(zz, 2).start()
 
     def rest(zz):
+        for m in (1, 2):
+            x_wait(zz, m)
+            y_wait(zz, m)
+        s_all(zz).start()
+
+    def rest_split(zz):
         x_wait(zz, 1)
         s_msg(zz, 1).start()
         y_wait(zz, 1)
@@ -206,8 +218,7 @@
             acc[:, n] += total
 
     def whole(zz):
-        for m in range(4):
-            s_wait(zz, m)
+        s_all_wait(zz)
 
     def some(zz, i, first=False):
         add_plane(zz, pl.ds(i * wide, wide), first)
@@ -226,7 +237,6 @@
         for m in (0, 1):
             x_msg(inner, m).start()
             y_msg(inner, m).start()
-        s_msg(inner, 0).start()
 
     @pl.when(jnp.logical_not(at_end))
     def _():
@@ -265,12 +275,13 @@
     low = z < NZ // 2
     last = jnp.where(low, NZ - 1, 0)
 
-    def arrive_far(zz, m):
+    def arrive_far(zz, m, to_sibling=False):
         z_wait(zz, m)
         if m == 0:
             x_msg(zz, 1).start()
             y_msg(zz, 1).start()
-            s_msg(zz, 0).start()
+            if to_sibling:
+                s_msg(zz, 0).start()
         elif m == 1:
             y_msg(zz, 2).start()
         else:
@@ -286,7 +297,7 @@
         whole(inner)
         for i in range(2):
             some(inner, i)
-        arrive_far(last, 0)
+        arrive_far(last, 0, True)
         rest(second)
         whole(second)
         arrive_far(last, 1)
@@ -328,8 +339,9 @@
         for i in range(2):
             some(z + 1, i)
 
-    rest(last)
-    whole(last)
+    rest_split(last)
+    for m in range(4):
+        s_wait(last, m)
 
     tile = s_d.shape[2]
     tiles = width // tile
@@ -371,46 +383,55 @@
         hop_x[i].wait_recv()
         s_y[i, hi] = part_y + r_d[i, hi]
         last_y[i].start()
+    for j in range(1, 2 * NZ):
+        e_msg(j).wait_send()
+    x_msg(z, 0).wait_send()
+    y_msg(z, 0).wait_send()
+
+    @pl.when(at_end)
+    def _():
+        x_msg(inner, 0).wait_send()
+        y_msg(inner, 0).wait_send()
+
+    for zz in range(NZ):
+        for m in range(3):
+            @pl.when(can_up & (z >= zz) & ((z != zz) | wide_up | (m == 0)))
+            def _():
+                z_msg(True, zz, m).wait_send()
+
+            @pl.when(can_down & (z <= zz) & ((z != zz) | wide_down | (m == 0)))
+            def _():
+                z_msg(False, zz, m).wait_send()
+        for m in (1, 2):
+            x_msg(zz, m).wait_send()
+            y_msg(zz, m).wait_send()
+
+        @pl.when(last == zz)
+        def _():
+            for m in range(4):
+                s_msg(zz, m).wait_send()
+
+        @pl.when(last != zz)
+        def _():
+            s_all(zz).wait_send()
     for i in range(tiles):
         n = slice(i * tile, (i + 1) * tile)
         dir_x[i].wait_recv()
         dir_y[i].wait_recv()
         out_ref[lo, n] = shifted(t0, 0, i) + r_1[i, lo]
         out_ref[hi, n] = shifted(t0, 1, i) + r_1[i, hi]
+    for group in (hop_y, hop_x, dir_x, dir_y):
+        for c in group:
+            c.wait_send()
     for i in range(tiles):
         n = slice(i * tile, (i + 1) * tile)
         last_x[i].wait_recv()
         out_ref[lo, n] += r_2[i, lo]
         last_y[i].wait_recv()
         out_ref[hi, n] += r_2[i, hi]
-
-    for group in (hop_y, hop_x, dir_x, dir_y, last_x, last_y):
+    for group in (last_x, last_y):
         for c in group:
             c.wait_send()
-    for j in range(1, 2 * NZ):
-        e_msg(j).wait_send()
-    x_msg(z, 0).wait_send()
-    y_msg(z, 0).wait_send()
-
-    @pl.when(at_end)
-    def _():
-        x_msg(inner, 0).wait_send()
-        y_msg(inner, 0).wait_send()
-
-    for zz in range(NZ):
-        for m in range(3):
-            @pl.when(can_up & (z >= zz) & ((z != zz) | wide_up | (m == 0)))
-            def _():
-                z_msg(True, zz, m).wait_send()
-
-            @pl.when(can_down & (z <= zz) & ((z != zz) | wide_down | (m == 0)))
-            def _():
-                z_msg(False, zz, m).wait_send()
-        for m in (1, 2):
-            x_msg(zz, m).wait_send()
-            y_msg(zz, m).wait_send()
-        for m in range(4):
-            s_msg(zz, m).wait_send()
 
 
 def on_device(newest, earlier, lag_matrices):

time: 67 us -> 67.9 us (1.013)
  Pallas kernels: 64.3 us -> 65.2 us
    pallas_call x1, Pallas kernels: 64.3 us -> 65.2 us  [on_device(): pl.pallas_call(kernel, out_shape=jax.ShapeDtypeStruct((steps, height), jn...]
where the time goes in v2:
time: 67.9 us; the launch traced here: 67.7 us
  Pallas kernels  65.2 us (96%)
  local copies, waits for them, and re-layouts  2.46 us (4%)
    pallas_call x1, Pallas kernels, on_device(): pl.pallas_call(kernel, out_shape=jax.ShapeDtypeStruct((steps, height), jn...  65.2 us
    unnamed x3, local copies, waits for them, and re-layouts  1.74 us

profile of v2, /device:TPU:0, one launch (start us, length us, event | category | flops | bytes accessed | tf_op | source)
XLA Modules:
  0.0 67.7 jit_solution(919424696108556359)
XLA Ops:
  0.0 0.7 %pad.4 = bf16[4,1024]{1,0:T(4,128)(2,1)S(1)} pad(bf16[3,1024]{1,0:T(4,128)(2,1)} %param.4, bf16[]{:T(256)} %constant.2.clone.1), padding=1_0x0_0 | pad | bytes 14338 | tf_op jit(solution)/shard_map/jit(_pad)/pad | solution.py:442
  0.7 0.0 copy-start
  0.7 0.9 %copy-done = bf16[128,1024]{1,0:T(8,128)(2,1)S(1)} copy-done((bf16[128,1024]{1,0:T(8,128)(2,1)S(1)}, bf16[128,1024]{1,0:T(8,128)(2,1)}, u32[]{:S(2)}) %copy-start) | copy-done | bytes 262168
  1.7 65.2 %shard_map.37 = f32[128,1024]{1,0:T(8,128)S(1)} custom-call(bf16[128,1024]{1,0:T(8,128)(2,1)S(1)} %copy-done, bf16[16,256]{1,0:T(8,128)(2,1)S(1)} %reshape.7.ear_ref, bf16[1,1024,8192]{2,1,0:T(8,128)(2,1)} %mat_ref.1), custom_call_target="tpu_custom_call" | custom-call | flops 8589934592 | bytes 16777216 | tf_op jit(solution)/shard_map/pallas_call | solution.py:449
  66.9 0.8 %copy.6 = f32[128,1024]{1,0:T(8,128)} copy(f32[128,1024]{1,0:T(8,128)S(1)} %shard_map.37) | data formatting | bytes 1048576
  (1 shorter events, 0.0 us)
Async XLA Ops:
  0.7 1.0 %copy-start = (bf16[128,1024]{1,0:T(8,128)(2,1)S(1)}, bf16[128,1024]{1,0:T(8,128)(2,1)}, u32[]{:S(2)}) copy-start(bf16[128,1024]{1,0:T(8,128)(2,1)} %new_ref.1) | copy-start | bytes 786436

commit v3 on v0

--- a/solution.py
+++ b/solution.py
@@ -423,7 +423,7 @@
     any_spec = pl.BlockSpec(memory_space=pl.ANY)
     vmem = pl.BlockSpec(memory_space=pltpu.VMEM)
     dma = pltpu.SemaphoreType.DMA
-    tile = 256
+    tile = 512
     block = pltpu.VMEM((height // tile, steps, tile), jnp.float32)
     return pl.pallas_call(
         kernel,

time: 67 us -> 66.8 us (level)
  no operation moved by 1% of the time
where the time goes in v3:
time: 66.8 us; the launch traced here: 66.6 us
  Pallas kernels  64.2 us (96%)
  local copies, waits for them, and re-layouts  2.46 us (4%)
    pallas_call x1, Pallas kernels, on_device(): pl.pallas_call(kernel, out_shape=jax.ShapeDtypeStruct((steps, height), jn...  64.2 us
    unnamed x3, local copies, waits for them, and re-layouts  1.74 us

profile of v3, /device:TPU:0, one launch (start us, length us, event | category | flops | bytes accessed | tf_op | source)
XLA Modules:
  0.0 66.6 jit_solution(17710412621217183452)
XLA Ops:
  0.0 0.7 %pad.4 = bf16[4,1024]{1,0:T(4,128)(2,1)S(1)} pad(bf16[3,1024]{1,0:T(4,128)(2,1)} %param.4, bf16[]{:T(256)} %constant.2.clone.1), padding=1_0x0_0 | pad | bytes 14338 | tf_op jit(solution)/shard_map/jit(_pad)/pad | solution.py:421
  0.7 0.0 copy-start
  0.7 0.9 %copy-done = bf16[128,1024]{1,0:T(8,128)(2,1)S(1)} copy-done((bf16[128,1024]{1,0:T(8,128)(2,1)S(1)}, bf16[128,1024]{1,0:T(8,128)(2,1)}, u32[]{:S(2)}) %copy-start) | copy-done | bytes 262168
  1.7 64.2 %shard_map.37 = f32[128,1024]{1,0:T(8,128)S(1)} custom-call(bf16[128,1024]{1,0:T(8,128)(2,1)S(1)} %copy-done, bf16[16,256]{1,0:T(8,128)(2,1)S(1)} %reshape.7.ear_ref, bf16[1,1024,8192]{2,1,0:T(8,128)(2,1)} %mat_ref.1), custom_call_target="tpu_custom_call" | custom-call | flops 8589934592 | bytes 16777216 | tf_op jit(solution)/shard_map/pallas_call | solution.py:428
  65.8 0.8 %copy.6 = f32[128,1024]{1,0:T(8,128)} copy(f32[128,1024]{1,0:T(8,128)S(1)} %shard_map.37) | data formatting | bytes 1048576
  (1 shorter events, 0.0 us)
Async XLA Ops:
  0.7 1.0 %copy-start = (bf16[128,1024]{1,0:T(8,128)(2,1)S(1)}, bf16[128,1024]{1,0:T(8,128)(2,1)}, u32[]{:S(2)}) copy-start(bf16[128,1024]{1,0:T(8,128)(2,1)} %new_ref.1) | copy-start | bytes 786436

commit v4 on v3

--- a/solution.py
+++ b/solution.py
@@ -280,9 +280,9 @@
     def _():
         second = jnp.where(low, 2, NZ - 3)
         arrive_far(second, 0)
-        rest(inner)
         arrive_far(second, 1)
         arrive_far(second, 2)
+        rest(inner)
         whole(inner)
         for i in range(2):
             some(inner, i)

time: 66.8 us -> 66.8 us (level)
  no operation moved by 1% of the time
where the time goes in v4:
time: 66.8 us; the launch traced here: 66.6 us
  Pallas kernels  64.2 us (96%)
  local copies, waits for them, and re-layouts  2.46 us (4%)
    pallas_call x1, Pallas kernels, on_device(): pl.pallas_call(kernel, out_shape=jax.ShapeDtypeStruct((steps, height), jn...  64.2 us
    unnamed x3, local copies, waits for them, and re-layouts  1.74 us

profile of v4, /device:TPU:0, one launch (start us, length us, event | category | flops | bytes accessed | tf_op | source)
XLA Modules:
  0.0 66.6 jit_solution(10973227562051526811)
XLA Ops:
  0.0 0.7 %pad.4 = bf16[4,1024]{1,0:T(4,128)(2,1)S(1)} pad(bf16[3,1024]{1,0:T(4,128)(2,1)} %param.4, bf16[]{:T(256)} %constant.2.clone.1), padding=1_0x0_0 | pad | bytes 14338 | tf_op jit(solution)/shard_map/jit(_pad)/pad | solution.py:421
  0.7 0.0 copy-start
  0.7 0.9 %copy-done = bf16[128,1024]{1,0:T(8,128)(2,1)S(1)} copy-done((bf16[128,1024]{1,0:T(8,128)(2,1)S(1)}, bf16[128,1024]{1,0:T(8,128)(2,1)}, u32[]{:S(2)}) %copy-start) | copy-done | bytes 262168
  1.7 64.2 %shard_map.37 = f32[128,1024]{1,0:T(8,128)S(1)} custom-call(bf16[128,1024]{1,0:T(8,128)(2,1)S(1)} %copy-done, bf16[16,256]{1,0:T(8,128)(2,1)S(1)} %reshape.7.ear_ref, bf16[1,1024,8192]{2,1,0:T(8,128)(2,1)} %mat_ref.1), custom_call_target="tpu_custom_call" | custom-call | flops 8589934592 | bytes 16777216 | tf_op jit(solution)/shard_map/pallas_call | solution.py:428
  65.8 0.8 %copy.6 = f32[128,1024]{1,0:T(8,128)} copy(f32[128,1024]{1,0:T(8,128)S(1)} %shard_map.37) | data formatting | bytes 1048576
  (1 shorter events, 0.0 us)
Async XLA Ops:
  0.7 1.0 %copy-start = (bf16[128,1024]{1,0:T(8,128)(2,1)S(1)}, bf16[128,1024]{1,0:T(8,128)(2,1)}, u32[]{:S(2)}) copy-start(bf16[128,1024]{1,0:T(8,128)(2,1)} %new_ref.1) | copy-start | bytes 786436
